TPU v7x, 128 devices: a whole 4x4x4 slice. The times are simulated.
128 devices in a mesh: rows: 64 (over x, z, y), cols: 2 (over core).
Axes of the slice: x: 4, y: 4, z: 4, core: 2. Of those that a mesh axis runs over, the one named last changes fastest.
Arguments:
- blocks: bfloat16 [4096, 7, 128, 128], P('rows'), may hold values from -0.1875 to 0.1875
- col_index: int32 [4096, 7], P('rows'), may hold values from 0 to 4095, as said below
- right_vecs: bfloat16 [64, 4096, 128], P('cols', 'rows'), may hold values from -30 to 30
- left_vecs: bfloat16 [64, 4096, 128], P('cols', 'rows'), may hold values from -30 to 30
- ritz: bfloat16 [64, 64], replicated, may hold values from -0.75 to 0.75
Outputs:
- right_res: float32 [64, 4096, 128], P('cols', 'rows')
- left_res: float32 [64, 4096, 128], P('cols', 'rows')
- right_norms: float32 [64], P('cols')
- left_norms: float32 [64], P('cols')
Inputs may be any that keep to these rules, and one draw needn't show every extreme that they name: `col_index`: entry 0 of each block row is the row's own index. Device p of rows holds block rows p * 64 to (p + 1) * 64 - 1. The devices form a grid of 2 x (32) subdomains of the slab, p = i * M + j with M = 32, periodic along j. Columns outside a device's own rows lie only on its three face neighbours: (i, j + 1 mod M), (i, j - 1 mod M) and (1 - i, j). Among the entries of one device's block rows exactly 2 have a column on (i, j + 1 mod M), and 1 to 2 on each of the other two.
All inputs are finite; a program needn't handle non-finite values.
Results may differ from a plain program's by a relative error of at most 0.0006.
Values may be sent and summed in bfloat16 or wider, within the bound.
A program may use at most 128 MiB of HBM per device.

v0:
```python
import jax
import jax.numpy as jnp
from jax import lax
from jax.sharding import PartitionSpec as P

SENDS = 2


def shards(blocks, col_index, right_vecs, left_vecs, ritz):
    peers = lax.axis_size("rows")
    me = lax.axis_index("rows")
    rows_here = col_index.shape[0]
    slots = col_index.shape[1]
    vec_here = right_vecs.shape[0]
    width = right_vecs.shape[2]
    owner = (col_index // rows_here).reshape(-1)
    local_id = (col_index % rows_here).reshape(-1)
    remote = owner != me
    onehot = (owner[:, None] == jnp.arange(peers, dtype=jnp.int32)[None, :]).astype(jnp.int32)
    rank = jnp.sum(jnp.cumsum(onehot, axis=0) * onehot, axis=1) - 1
    ext_index = jnp.where(remote, rows_here + owner * SENDS + rank, local_id)
    target = jnp.where(remote, owner, peers)
    wanted = jnp.zeros((peers, SENDS), jnp.int32).at[target, rank].set(local_id, mode="drop")
    asked = lax.all_to_all(wanted, "rows", split_axis=0, concat_axis=0, tiled=True)
    asked_flat = asked.reshape(-1)
    outgoing = right_vecs[:, asked_flat, :]
    contrib = jnp.einsum("kra,rsab->krsb", left_vecs, blocks, preferred_element_type=jnp.float32)
    contrib = contrib.reshape(vec_here, rows_here * slots, width)
    summed = (
        jnp.zeros((vec_here, rows_here + peers * SENDS, width), jnp.float32)
        .at[:, ext_index, :]
        .add(contrib)
    )
    incoming = lax.all_to_all(outgoing, "rows", split_axis=1, concat_axis=1, tiled=True)
    returned = lax.all_to_all(
        summed[:, rows_here:, :].astype(jnp.bfloat16),
        "rows",
        split_axis=1,
        concat_axis=1,
        tiled=True,
    ).astype(jnp.float32)
    extended = jnp.concatenate([right_vecs, incoming], axis=1)
    gathered = extended[:, ext_index, :].reshape(vec_here, rows_here, slots, width)
    product = jnp.einsum("krsj,rsij->kri", gathered, blocks, preferred_element_type=jnp.float32)
    transposed = summed[:, :rows_here, :].at[:, asked_flat, :].add(returned)
    mine = lax.axis_index("cols") * vec_here
    full_right, full_left = (
        lax.all_gather(right_vecs, "cols", axis=0, tiled=True),
        lax.all_gather(left_vecs, "cols", axis=0, tiled=True),
    )
    total = ritz.shape[0]
    right_table = lax.dynamic_slice(ritz, (0, mine), (total, vec_here))
    left_table = lax.dynamic_slice(ritz.T, (0, mine), (total, vec_here))
    right_shift = jnp.einsum(
        "krb,kq->qrb", full_right, right_table, preferred_element_type=jnp.float32
    )
    left_shift = jnp.einsum(
        "krb,kq->qrb", full_left, left_table, preferred_element_type=jnp.float32
    )
    right_res = product - right_shift
    left_res = transposed - left_shift
    right_sq, left_sq = lax.psum(
        (jnp.sum(right_res * right_res, axis=(1, 2)), jnp.sum(left_res * left_res, axis=(1, 2))),
        "rows",
    )
    return (right_res, left_res, jnp.sqrt(right_sq), jnp.sqrt(left_sq))


def solution(mesh):
    placed = (
        P("rows", None, None, None),
        P("rows", None),
        P("cols", "rows", None),
        P("cols", "rows", None),
        P(),
    )
    return jax.shard_map(
        shards,
        mesh=mesh,
        in_specs=placed,
        out_specs=(P("cols", "rows", None), P("cols", "rows", None), P("cols"), P("cols")),
        check_vma=False,
    )
```

profile of v0, /device:TPU:0, one launch (start us, length us, event | category | flops | bytes accessed | tf_op | source)
XLA Modules:
  0.0 374.0 jit_solution(11511773437690598463)
XLA Ops:
  7.2 0.8 add_select_fusion
  8.8 1.2 reduce-window.6
  10.4 21.3 %scatter_fusion = s32[64,2]{0,1:T(2,128)S(1)} fusion(s32[64,2]{0,1:T(2,128)S(1)} %broadcast_in_dim.8, s32[448]{0:T(512)S(1)} %bitcast.54, s32[448]{0:T(512)S(1)} %reshape.185), kind=kCustom, calls=%fused_computation.2 | custom fusion | bytes 8960 | tf_op jit(solution)/shard_map/scatter | solution.py:23
  31.8 0.7 copy.36
  32.5 11.5 %all-to-all-start = ((s32[64,1,2]{2,1,0:T(1,128)}), s32[64,1,2]{2,1,0:T(1,128)S(1)}, u32[]{:S(2)}, u32[]{:S(2)}) async-start(s32[64,1,2]{2,1,0:T(1,128)} %copy.36), calls=%async_computation | async-start | bytes 65536 | tf_op jit(solution)/shard_map/all_to_all | solution.py:24
  44.0 10.5 %fusion = f32[64,7,128,32]{2,3,1,0:T(8,128)} fusion(bf16[64,7,128,128]{3,2,1,0:T(8,128)(2,1)} %param.5, bf16[32,64,128,1]{2,1,0,3:T(8,128)(2,1)S(1)} %bitcast.57), kind=kOutput, calls=%fused_computation.13 | convolution fusion | flops 469762048 | bytes 22544384 | tf_op jit(solution)/shard_map/kra,rsab->krsb/dot_general | solution.py:27
  54.5 2.1 broadcast_in_dim.10
  56.6 59.6 %scatter_fusion.1 = f32[32,192,128]{2,0,1:T(8,128)} fusion(f32[32,192,128]{2,0,1:T(8,128)} %broadcast_in_dim.10, s32[448]{0:T(512)S(1)} %bitcast.58, f32[448,32,128]{2,1,0:T(8,128)} %bitcast.53), kind=kCustom, calls=%fused_computation.3 | custom fusion | flops 1835008 | bytes 22021888 | tf_op jit(solution)/shard_map/scatter-add | solution.py:32
  116.2 2.8 slice.36
  119.0 10.3 %all-to-all-start.2 = ((bf16[32,128,128]{2,0,1:T(8,128)(2,1)}), bf16[32,128,128]{2,0,1:T(8,128)(2,1)S(1)}, u32[]{:S(2)}, u32[]{:S(2)}) async-start(bf16[32,128,128]{2,0,1:T(8,128)(2,1)} %slice.36), calls=%async_computation.2 | async-start | bytes 2097152 | tf_op jit(solution)/shard_map/all_to_all | solution.py:35
  129.6 1.1 copy.43
  130.8 0.5 broadcast.201
  131.3 0.7 reduce.5
  132.2 5.2 %gather_fusion = bf16[128,32,128]{2,0,1:T(8,128)(2,1)S(1)} fusion(bf16[32,64,128]{2,1,0:T(8,128)(2,1)S(1)} %copy-done.1, s32[1024]{0:T(1024)S(1)} %pad_clamp_fusion.1), kind=kCustom, calls=%fused_computation | custom fusion | bytes 2097664 | tf_op jit(solution)/shard_map/gather | solution.py:26
  137.4 1.6 copy.37
  139.0 8.3 %all-to-all-done.2 = bf16[32,128,128]{2,0,1:T(8,128)(2,1)S(1)} async-done(((bf16[32,128,128]{2,0,1:T(8,128)(2,1)}), bf16[32,128,128]{2,0,1:T(8,128)(2,1)S(1)}, u32[]{:S(2)}, u32[]{:S(2)}) %all-to-all-start.2) | async-done | bytes 1048608 | tf_op jit(solution)/shard_map/all_to_all | solution.py:35
  147.3 5.5 %all-to-all-start.1 = ((bf16[32,128,128]{2,0,1:T(8,128)(2,1)}), bf16[32,128,128]{2,0,1:T(8,128)(2,1)}, u32[]{:S(2)}, u32[]{:S(2)}) async-start(bf16[32,128,128]{2,0,1:T(8,128)(2,1)} %copy.37), calls=%async_computation.1 | async-start | bytes 2097152 | tf_op jit(solution)/shard_map/all_to_all | solution.py:34
  152.9 1.2 copy.38
  154.1 1.3 slice.29
  155.4 1.5 convert_bitcast_fusion
  156.9 5.9 %scatter_fusion.2 = f32[32,64,128]{2,0,1:T(8,128)S(1)} fusion(f32[32,64,128]{2,0,1:T(8,128)S(1)} %slice.29, s32[128]{0:T(128)S(1)} %fusion.10, f32[128,32,128]{2,1,0:T(8,128)S(1)} %convert_bitcast_fusion), kind=kCustom, calls=%fused_computation.4 | custom fusion | flops 524288 | bytes 6291968 | tf_op jit(solution)/shard_map/scatter-add | solution.py:45
  162.9 6.7 %all-to-all-done.1 = bf16[32,128,128]{2,0,1:T(8,128)(2,1)} async-done(((bf16[32,128,128]{2,0,1:T(8,128)(2,1)}), bf16[32,128,128]{2,0,1:T(8,128)(2,1)}, u32[]{:S(2)}, u32[]{:S(2)}) %all-to-all-start.1) | async-done | bytes 1048608 | tf_op jit(solution)/shard_map/all_to_all | solution.py:34
  169.6 1.5 pad_maximum_fusion
  171.1 3.4 gather_fusion.1
  174.4 11.4 %convolution_bitcast_fusion = f32[32,64,128]{2,0,1:T(8,128)S(1)} fusion(bf16[32,64,7,128]{3,0,2,1:T(8,128)(2,1)} %bitcast.55, bf16[64,7,128,128]{3,2,1,0:T(8,128)(2,1)} %param.5), kind=kOutput, calls=%fused_computation.10 | convolution fusion | flops 469762048 | bytes 19398656 | tf_op jit(solution)/shard_map/krsj,rsij->kri/dot_general | solution.py:44
  185.9 1.6 multiply_reduce_fusion
  187.6 1.7 multiply_reduce_fusion.1
  189.3 173.7 %all-reduce.1 = (f32[32]{0:T(128)S(1)}, f32[32]{0:T(128)S(1)}) all-reduce(f32[32]{0:T(128)S(1)} %get-tuple-element.24, f32[32]{0:T(128)S(1)} %get-tuple-element.26), channel_id=1, replica_groups=mesh['rows'=64,'cols'=2] {'rows'}, use_global_device_ids=true, to_apply=%region_7.8 | all-reduce | flops 64 | bytes 512 | tf_op jit(solution)/shard_map/psum | solution.py:62
  363.0 0.5 sqrt.6
  363.5 0.5 sqrt.7
  364.0 1.6 copy.45
  365.6 1.6 copy.44
  (35 shorter events, 1.7 us)
Async XLA Ops:
  7.2 178.7 %copy-start = (bf16[64,64]{1,0:T(8,128)(2,1)S(1)}, bf16[64,64]{1,0:T(8,128)(2,1)}, u32[]{:S(2)}) copy-start(bf16[64,64]{1,0:T(8,128)(2,1)} %param.9) | copy-start | bytes 24580
  7.2 36.8 %copy-start.3 = (bf16[32,64,128]{2,1,0:T(8,128)(2,1)S(1)}, bf16[32,64,128]{2,1,0:T(8,128)(2,1)}, u32[]{:S(2)}) copy-start(bf16[32,64,128]{2,1,0:T(8,128)(2,1)} %param.8) | copy-start | bytes 1572868
  32.5 86.6 %all-to-all-start = ((s32[64,1,2]{2,1,0:T(1,128)}), s32[64,1,2]{2,1,0:T(1,128)S(1)}, u32[]{:S(2)}, u32[]{:S(2)}) async-start(s32[64,1,2]{2,1,0:T(1,128)} %copy.36), calls=%async_computation | async-start | bytes 65536 | tf_op jit(solution)/shard_map/all_to_all | solution.py:24
  116.2 16.0 %copy-start.1 = (bf16[32,64,128]{2,1,0:T(8,128)(2,1)S(1)}, bf16[32,64,128]{2,1,0:T(8,128)(2,1)}, u32[]{:S(2)}) copy-start(bf16[32,64,128]{2,1,0:T(8,128)(2,1)} %param.7) | copy-start | bytes 1572868
  119.0 28.3 %all-to-all-start.2 = ((bf16[32,128,128]{2,0,1:T(8,128)(2,1)}), bf16[32,128,128]{2,0,1:T(8,128)(2,1)S(1)}, u32[]{:S(2)}, u32[]{:S(2)}) async-start(bf16[32,128,128]{2,0,1:T(8,128)(2,1)} %slice.36), calls=%async_computation.2 | async-start | bytes 2097152 | tf_op jit(solution)/shard_map/all_to_all | solution.py:35
  129.4 56.5 %all-gather.5.cloned.1.call-start = ((), (), s32[]{:S(2)}) async-start(), calls=%async_computation.4 | async-start | bytes 1572864 | tf_op jit(solution)/shard_map/all_gather | solution.py:49
  147.3 6.7 %copy-start.2 = (bf16[32,128,128]{2,0,1:T(8,128)(2,1)}, bf16[32,128,128]{2,0,1:T(8,128)(2,1)S(1)}, u32[]{:S(2)}) copy-start(bf16[32,128,128]{2,0,1:T(8,128)(2,1)S(1)} %all-to-all-done.2) | copy-start | bytes 3145732
  147.3 22.2 %all-to-all-start.1 = ((bf16[32,128,128]{2,0,1:T(8,128)(2,1)}), bf16[32,128,128]{2,0,1:T(8,128)(2,1)}, u32[]{:S(2)}, u32[]{:S(2)}) async-start(bf16[32,128,128]{2,0,1:T(8,128)(2,1)} %copy.37), calls=%async_computation.1 | async-start | bytes 2097152 | tf_op jit(solution)/shard_map/all_to_all | solution.py:34
  152.9 34.7 %all-gather.3.cloned.1.call-start = ((), (), s32[]{:S(2)}) async-start(), calls=%async_computation.3 | async-start | bytes 1572864 | tf_op jit(solution)/shard_map/all_gather | solution.py:48
Sparse Core Ops, SparseCore 0:
  131.9 12.9 all-gather.4
  155.4 12.9 all-gather.2
where the time goes:
time: 375 us; the launch traced here: 374 us
  blocking collectives  174 us (46%)
  other arithmetic  71.5 us (19%)
  local copies, waits for them, and re-layouts  46.6 us (12%)
  starting transfers between devices  27.6 us (7%)
  matrix products  25.3 us (7%)
  waiting for transfers between devices  15.1 us (4%)
  between operations  14.3 us (4%)
    psum x1, blocking collectives, shards(): lax.psum((jnp.sum(right_res * right_res, axis=(1, 2)), jnp.sum(left_res *...  174 us
    scatter-add x1, other arithmetic, shards(): summed = jnp.zeros((vec_here, rows_here + peers * SENDS, width), jnp.floa...  59.6 us
    scatter x1, local copies, waits for them, and re-layouts, shards(): jnp.zeros((peers, SENDS), jnp.int32).at[target, rank]  21.3 us
    all_to_all x1, starting transfers between devices, shards(): lax.all_to_all(wanted, 'rows', split_axis=0, concat_axis=0, tiled=True)  11.5 us
    dot_general x1, matrix products, shards(): jnp.einsum('krsj,rsij->kri', gathered, blocks, preferred_element_type=jnp...  11.4 us
    dot_general x1, matrix products, shards(): jnp.einsum('kra,rsab->krsb', left_vecs, blocks, preferred_element_type=jn...  10.5 us
    all_to_all x1, starting transfers between devices, shards(): lax.all_to_all(summed[:, rows_here:, :].astype(jnp.bfloat16), 'rows', spl...  10.3 us
    all_to_all x1, waiting for transfers between devices, shards(): lax.all_to_all(summed[:, rows_here:, :].astype(jnp.bfloat16), 'rows', spl...  8.32 us
  transfers between devices with their start and end apart: 5, of which 2 were waited for; matrix products, arithmetic and copies ran while one was open for 30% of the time, Pallas kernels for 0%

commit v1 on v0

--- a/solution.py
+++ b/solution.py
@@ -4,6 +4,18 @@
 from jax.sharding import PartitionSpec as P
 
 SENDS = 2
+
+
+def block_run(local_x, a_name):
+    return jnp.concatenate(
+        lax.all_to_all(
+            jnp.stack(jnp.split(local_x, lax.axis_size(a_name), 1)),
+            split_axis=0,
+            concat_axis=0,
+            axis_name=a_name,
+        ),
+        1,
+    )
 
 
 def shards(blocks, col_index, right_vecs, left_vecs, ritz):
@@ -32,13 +44,7 @@
         .add(contrib)
     )
     incoming = lax.all_to_all(outgoing, "rows", split_axis=1, concat_axis=1, tiled=True)
-    returned = lax.all_to_all(
-        summed[:, rows_here:, :].astype(jnp.bfloat16),
-        "rows",
-        split_axis=1,
-        concat_axis=1,
-        tiled=True,
-    ).astype(jnp.float32)
+    returned = block_run(summed[:, rows_here:, :].astype(jnp.bfloat16), "rows").astype(jnp.float32)
     extended = jnp.concatenate([right_vecs, incoming], axis=1)
     gathered = extended[:, ext_index, :].reshape(vec_here, rows_here, slots, width)
     product = jnp.einsum("krsj,rsij->kri", gathered, blocks, preferred_element_type=jnp.float32)

time: 375 us -> 392 us (1.045)
  local copies, waits for them, and re-layouts: 46.6 us -> 82.2 us
  other arithmetic: 71.5 us -> 52.2 us
    unnamed x12 -> x79, local copies, waits for them, and re-layouts: 5.47 us -> 45 us
    scatter-add x1, other arithmetic: 59.6 us -> 40 us  [shards(): summed = jnp.zeros((vec_here, rows_here + peers * SENDS, width), jnp.floa...]
  transfers between devices with their start and end apart: 5 -> 5, of which waited for: 2 -> 2; matrix products, arithmetic and copies ran while one was open for 30% -> 33% of each run, Pallas kernels for 0% -> 0%
where the time goes in v1:
time: 392 us; the launch traced here: 390 us
  blocking collectives  174 us (44%)
  local copies, waits for them, and re-layouts  82.2 us (21%)
  other arithmetic  52.2 us (13%)
  starting transfers between devices  27.7 us (7%)
  matrix products  25.3 us (6%)
  waiting for transfers between devices  15 us (4%)
  between operations  14.3 us (4%)
    psum x1, blocking collectives, shards(): lax.psum((jnp.sum(right_res * right_res, axis=(1, 2)), jnp.sum(left_res *...  174 us
    unnamed x79, local copies, waits for them, and re-layouts  45 us
    scatter-add x1, other arithmetic, shards(): summed = jnp.zeros((vec_here, rows_here + peers * SENDS, width), jnp.floa...  40 us
    scatter x1, local copies, waits for them, and re-layouts, shards(): jnp.zeros((peers, SENDS), jnp.int32).at[target, rank]  21.3 us
    all_to_all x1, starting transfers between devices, shards(): lax.all_to_all(wanted, 'rows', split_axis=0, concat_axis=0, tiled=True)  11.5 us
    dot_general x1, matrix products, shards(): jnp.einsum('krsj,rsij->kri', gathered, blocks, preferred_element_type=jnp...  11.4 us
    dot_general x1, matrix products, shards(): jnp.einsum('kra,rsab->krsb', left_vecs, blocks, preferred_element_type=jn...  10.5 us
    all_to_all x1, starting transfers between devices, block_run(): lax.all_to_all(jnp.stack(jnp.split(local_x, lax.axis_size(a_name), 1)), s...  10.4 us
  transfers between devices with their start and end apart: 5, of which 2 were waited for; matrix products, arithmetic and copies ran while one was open for 33% of the time, Pallas kernels for 0%

profile of v1, /device:TPU:0, one launch (start us, length us, event | category | flops | bytes accessed | tf_op | source)
XLA Modules:
  0.0 390.5 jit_solution(649903157686062535)
XLA Ops:
  7.2 0.7 add_select_fusion
  8.7 1.2 reduce-window.6
  10.4 21.3 %scatter_fusion = s32[64,2]{0,1:T(2,128)S(1)} fusion(s32[64,2]{0,1:T(2,128)S(1)} %broadcast_in_dim.8, s32[448]{0:T(512)S(1)} %bitcast.313, s32[448]{0:T(512)S(1)} %reshape.190), kind=kCustom, calls=%fused_computation.2 | custom fusion | bytes 8960 | tf_op jit(solution)/shard_map/scatter | solution.py:35
  31.7 0.7 copy.36
  32.4 11.5 %all-to-all-start = ((s32[64,1,2]{2,1,0:T(1,128)}), s32[64,1,2]{2,1,0:T(1,128)S(1)}, u32[]{:S(2)}, u32[]{:S(2)}) async-start(s32[64,1,2]{2,1,0:T(1,128)} %copy.36), calls=%async_computation | async-start | bytes 65536 | tf_op jit(solution)/shard_map/all_to_all | solution.py:36
  43.9 10.5 %fusion = f32[64,7,128,32]{2,3,1,0:T(8,128)} fusion(bf16[64,7,128,128]{3,2,1,0:T(8,128)(2,1)} %param.5, bf16[32,64,128,1]{2,1,0,3:T(8,128)(2,1)S(1)} %bitcast.317), kind=kOutput, calls=%fused_computation.11 | convolution fusion | flops 469762048 | bytes 22544384 | tf_op jit(solution)/shard_map/kra,rsab->krsb/dot_general | solution.py:39
  54.8 40.0 %scatter_fusion.1 = f32[32,192,128]{2,0,1:T(8,128)S(1)} fusion(f32[32,192,128]{2,0,1:T(8,128)S(1)} %broadcast_in_dim.10, s32[448]{0:T(512)S(1)} %bitcast.318, f32[448,32,128]{2,1,0:T(8,128)} %bitcast.312), kind=kCustom, calls=%fused_computation.3 | custom fusion | flops 1835008 | bytes 22021888 | tf_op jit(solution)/shard_map/scatter-add | solution.py:44
  95.2 1.3 copy-done.2
  96.5 0.6 constant_dynamic-update-slice_fusion.63
  97.1 0.6 constant_dynamic-update-slice_fusion.62
  97.7 0.6 constant_dynamic-update-slice_fusion.61
  98.3 0.6 constant_dynamic-update-slice_fusion.60
  135.4 10.4 %all-to-all-start.2 = ((bf16[64,32,2,128]{3,1,2,0:T(8,128)(2,1)}), bf16[64,32,2,128]{3,1,2,0:T(8,128)(2,1)S(1)}, u32[]{:S(2)}, u32[]{:S(2)}) async-start(bf16[64,32,2,128]{3,1,2,0:T(8,128)(2,1)} %constant_dynamic-update-slice_fusion), calls=%async_computation.2 | async-start | bytes 2097152 | tf_op jit(solution)/shard_map/all_to_all | solution.py:11
  146.0 1.2 copy.43
  147.7 0.7 reduce.5
  148.6 5.2 %gather_fusion = bf16[128,32,128]{2,0,1:T(8,128)(2,1)S(1)} fusion(bf16[32,64,128]{2,1,0:T(8,128)(2,1)S(1)} %copy-done.1, s32[1024]{0:T(1024)S(1)} %pad_clamp_fusion.1), kind=kCustom, calls=%fused_computation | custom fusion | bytes 2097664 | tf_op jit(solution)/shard_map/gather | solution.py:38
  153.8 1.6 copy.37
  155.5 8.3 %all-to-all-done.2 = bf16[64,32,2,128]{3,1,2,0:T(8,128)(2,1)S(1)} async-done(((bf16[64,32,2,128]{3,1,2,0:T(8,128)(2,1)}), bf16[64,32,2,128]{3,1,2,0:T(8,128)(2,1)S(1)}, u32[]{:S(2)}, u32[]{:S(2)}) %all-to-all-start.2) | async-done | bytes 1048608 | tf_op jit(solution)/shard_map/all_to_all | solution.py:11
  163.8 5.5 %all-to-all-start.1 = ((bf16[32,128,128]{2,0,1:T(8,128)(2,1)}), bf16[32,128,128]{2,0,1:T(8,128)(2,1)}, u32[]{:S(2)}, u32[]{:S(2)}) async-start(bf16[32,128,128]{2,0,1:T(8,128)(2,1)} %copy.37), calls=%async_computation.1 | async-start | bytes 2097152 | tf_op jit(solution)/shard_map/all_to_all | solution.py:46
  169.3 1.2 copy.38
  170.5 1.3 slice.90
  171.8 1.5 convert_element_type.16
  173.4 5.9 %scatter_fusion.2 = f32[32,64,128]{2,0,1:T(8,128)S(1)} fusion(f32[32,64,128]{2,0,1:T(8,128)S(1)} %slice.90, s32[128]{0:T(128)S(1)} %fusion.10, f32[128,32,128]{2,1,0:T(8,128)S(1)} %bitcast.315), kind=kCustom, calls=%fused_computation.4 | custom fusion | flops 524288 | bytes 6291968 | tf_op jit(solution)/shard_map/scatter-add | solution.py:51
  179.3 6.7 %all-to-all-done.1 = bf16[32,128,128]{2,0,1:T(8,128)(2,1)} async-done(((bf16[32,128,128]{2,0,1:T(8,128)(2,1)}), bf16[32,128,128]{2,0,1:T(8,128)(2,1)}, u32[]{:S(2)}, u32[]{:S(2)}) %all-to-all-start.1) | async-done | bytes 1048608 | tf_op jit(solution)/shard_map/all_to_all | solution.py:46
  186.0 1.5 pad_maximum_fusion
  187.5 3.4 gather_fusion.1
  190.8 11.4 %convolution_bitcast_fusion = f32[32,64,128]{2,0,1:T(8,128)S(1)} fusion(bf16[32,64,7,128]{3,0,2,1:T(8,128)(2,1)} %bitcast.314, bf16[64,7,128,128]{3,2,1,0:T(8,128)(2,1)} %param.5), kind=kOutput, calls=%fused_computation.8 | convolution fusion | flops 469762048 | bytes 19398656 | tf_op jit(solution)/shard_map/krsj,rsij->kri/dot_general | solution.py:50
  202.3 1.6 multiply_reduce_fusion
  204.0 1.7 multiply_reduce_fusion.1
  205.7 173.7 %all-reduce.1 = (f32[32]{0:T(128)S(1)}, f32[32]{0:T(128)S(1)}) all-reduce(f32[32]{0:T(128)S(1)} %get-tuple-element.24, f32[32]{0:T(128)S(1)} %get-tuple-element.26), channel_id=1, replica_groups=mesh['rows'=64,'cols'=2] {'rows'}, use_global_device_ids=true, to_apply=%region_7.8 | all-reduce | flops 64 | bytes 512 | tf_op jit(solution)/shard_map/psum | solution.py:68
  380.5 1.6 copy.45
  382.0 1.6 copy.44
  (103 shorter events, 40.4 us)
Async XLA Ops:
  7.2 195.1 %copy-start = (bf16[64,64]{1,0:T(8,128)(2,1)S(1)}, bf16[64,64]{1,0:T(8,128)(2,1)}, u32[]{:S(2)}) copy-start(bf16[64,64]{1,0:T(8,128)(2,1)} %param.9) | copy-start | bytes 24580
  10.4 33.5 %copy-start.4 = (bf16[32,64,128]{2,1,0:T(8,128)(2,1)S(1)}, bf16[32,64,128]{2,1,0:T(8,128)(2,1)}, u32[]{:S(2)}) copy-start(bf16[32,64,128]{2,1,0:T(8,128)(2,1)} %param.8) | copy-start | bytes 1572868
  32.4 102.9 %all-to-all-start = ((s32[64,1,2]{2,1,0:T(1,128)}), s32[64,1,2]{2,1,0:T(1,128)S(1)}, u32[]{:S(2)}, u32[]{:S(2)}) async-start(s32[64,1,2]{2,1,0:T(1,128)} %copy.36), calls=%async_computation | async-start | bytes 65536 | tf_op jit(solution)/shard_map/all_to_all | solution.py:36
  94.8 1.7 copy-start.2
  115.9 30.1 %copy-start.5 = (bf16[32,64,128]{2,1,0:T(8,128)(2,1)S(1)}, bf16[32,64,128]{2,1,0:T(8,128)(2,1)}, u32[]{:S(2)}) copy-start(bf16[32,64,128]{2,1,0:T(8,128)(2,1)} %param.8) | copy-start | bytes 1572868
  135.3 13.3 %copy-start.1 = (bf16[32,64,128]{2,1,0:T(8,128)(2,1)S(1)}, bf16[32,64,128]{2,1,0:T(8,128)(2,1)}, u32[]{:S(2)}) copy-start(bf16[32,64,128]{2,1,0:T(8,128)(2,1)} %param.7) | copy-start | bytes 1572868
  135.4 28.4 %all-to-all-start.2 = ((bf16[64,32,2,128]{3,1,2,0:T(8,128)(2,1)}), bf16[64,32,2,128]{3,1,2,0:T(8,128)(2,1)S(1)}, u32[]{:S(2)}, u32[]{:S(2)}) async-start(bf16[64,32,2,128]{3,1,2,0:T(8,128)(2,1)} %constant_dynamic-update-slice_fusion), calls=%async_computation.2 | async-start | bytes 2097152 | tf_op jit(solution)/shard_map/all_to_all | solution.py:11
  145.8 56.5 %all-gather.5.cloned.1.call-start = ((), (), s32[]{:S(2)}) async-start(), calls=%async_computation.4 | async-start | bytes 1572864 | tf_op jit(solution)/shard_map/all_gather | solution.py:55
  163.8 6.7 %copy-start.3 = (bf16[64,32,2,128]{3,1,2,0:T(8,128)(2,1)}, bf16[64,32,2,128]{3,1,2,0:T(8,128)(2,1)S(1)}, u32[]{:S(2)}) copy-start(bf16[64,32,2,128]{3,1,2,0:T(8,128)(2,1)S(1)} %all-to-all-done.2) | copy-start | bytes 3145732
  163.8 22.2 %all-to-all-start.1 = ((bf16[32,128,128]{2,0,1:T(8,128)(2,1)}), bf16[32,128,128]{2,0,1:T(8,128)(2,1)}, u32[]{:S(2)}, u32[]{:S(2)}) async-start(bf16[32,128,128]{2,0,1:T(8,128)(2,1)} %copy.37), calls=%async_computation.1 | async-start | bytes 2097152 | tf_op jit(solution)/shard_map/all_to_all | solution.py:46
  169.3 34.7 %all-gather.3.cloned.1.call-start = ((), (), s32[]{:S(2)}) async-start(), calls=%async_computation.3 | async-start | bytes 1572864 | tf_op jit(solution)/shard_map/all_gather | solution.py:54
Sparse Core Ops, SparseCore 0:
  148.3 12.9 all-gather.4
  171.8 12.9 all-gather.2
